TPU v7x, 256 devices: a whole 4x4x8 slice. The times are simulated.
256 devices in a mesh: rows: 32 (over y, x, core), cols: 8 (over z).
Axes of the slice: x: 4, y: 4, z: 8, core: 2. Of those that a mesh axis runs over, the one named last changes fastest.
Arguments:
- latent: float32 [2048, 16384], P('rows', 'cols'), may hold values from -3 to 3
- counts: int32 [2048, 16384], P('rows', 'cols'), may hold values from 0 to 39
- exposure: int32 [2048, 16384], P('rows', 'cols'), may hold values from 1 to 32
Outputs:
- newton_step: float32 [2048, 16384], P('rows', 'cols')
- residual: float32 [2048, 16384], P('rows', 'cols')
- direction: float32 [2048, 16384], P('rows', 'cols')
All inputs are finite; a program needn't handle non-finite values.
Results may differ from a plain program's by a relative error of at most 0.0003.
Values sent between devices are 32-bit elements; how exact they have to be, the bound alone decides.
No kernel may reach another device: no remote copies, remote signals or barrier semaphores. Data moves between devices by JAX's collectives and lax.ppermute only.
A program may use at most 128 MiB of HBM per device.

v0:
```python
import math
import jax
import jax.numpy as jnp
from jax import lax
from jax.sharding import PartitionSpec as P

dispersion = 4.0
prior_scale = 0.25
kappa_sq = 0.05
weight_shift = 1.0
highest = lax.Precision.HIGHEST


def extended(cells, sides, width):
    for axis, dim in sides:
        count = lax.axis_size(axis)
        ends = count - 1
        head = lax.slice_in_dim(cells, 0, width, axis=dim)
        tail = lax.slice_in_dim(cells, cells.shape[dim] - width, cells.shape[dim], axis=dim)
        cells = jnp.concatenate(
            [
                lax.ppermute(tail, axis, [(i, (i + 1) % count) for i in range(ends)]),
                cells,
                lax.ppermute(head, axis, [((i + 1) % count, i) for i in range(ends)]),
            ],
            axis=dim,
        )
    return cells


def dft_table(length):
    index_line = lax.iota(jnp.int32, length)
    product = index_line[:, None] * index_line[None, :] % length
    angle = 2.0 * math.pi / length * product.astype(jnp.float32)
    return (jnp.cos(angle), jnp.sin(angle))


def twiddle_table(outer_len, inner_len):
    product = lax.iota(jnp.int32, outer_len)[:, None] * lax.iota(jnp.int32, inner_len)[None, :]
    angle = 2.0 * math.pi / (outer_len * inner_len) * product.astype(jnp.float32)
    return (jnp.cos(angle), jnp.sin(angle))


def left_apply(table, data):
    return jnp.dot(table, data, precision=highest)


def middle_apply(table, data):
    return jnp.einsum("ka,lab->lkb", table, data, precision=highest)


def last_apply(data, table):
    line_rows, outer_len, inner_len = data.shape
    flat = jnp.dot(data.reshape(line_rows * outer_len, inner_len), table, precision=highest)
    return flat.reshape(line_rows, outer_len, inner_len)


def split_lengths(total_cols):
    inner_len = math.gcd(total_cols, 128)
    return (total_cols // inner_len, inner_len)


def columns_forward(real_part, imag_part):
    line_rows, total_cols = real_part.shape
    outer_len, inner_len = split_lengths(total_cols)
    outer_cos, outer_sin = dft_table(outer_len)
    inner_cos, inner_sin = dft_table(inner_len)
    twist_cos, twist_sin = twiddle_table(outer_len, inner_len)
    real_cube = real_part.reshape(line_rows, outer_len, inner_len)
    imag_cube = imag_part.reshape(line_rows, outer_len, inner_len)
    section_real = middle_apply(outer_cos, real_cube) + middle_apply(outer_sin, imag_cube)
    section_imag = middle_apply(outer_cos, imag_cube) - middle_apply(outer_sin, real_cube)
    turned_real = section_real * twist_cos + section_imag * twist_sin
    turned_imag = section_imag * twist_cos - section_real * twist_sin
    final_real = last_apply(turned_real, inner_cos) + last_apply(turned_imag, inner_sin)
    final_imag = last_apply(turned_imag, inner_cos) - last_apply(turned_real, inner_sin)
    return (final_real.reshape(line_rows, total_cols), final_imag.reshape(line_rows, total_cols))


def columns_inverse(real_part, imag_part):
    line_rows, total_cols = real_part.shape
    outer_len, inner_len = split_lengths(total_cols)
    outer_cos, outer_sin = dft_table(outer_len)
    inner_cos, inner_sin = dft_table(inner_len)
    twist_cos, twist_sin = twiddle_table(outer_len, inner_len)
    real_cube = real_part.reshape(line_rows, outer_len, inner_len)
    imag_cube = imag_part.reshape(line_rows, outer_len, inner_len)
    section_real = last_apply(real_cube, inner_cos) - last_apply(imag_cube, inner_sin)
    section_imag = last_apply(imag_cube, inner_cos) + last_apply(real_cube, inner_sin)
    turned_real = section_real * twist_cos - section_imag * twist_sin
    turned_imag = section_imag * twist_cos + section_real * twist_sin
    final_real = middle_apply(outer_cos, turned_real) - middle_apply(outer_sin, turned_imag)
    final_imag = middle_apply(outer_cos, turned_imag) + middle_apply(outer_sin, turned_real)
    return (final_real.reshape(line_rows, total_cols), final_imag.reshape(line_rows, total_cols))


def inverse_symbol(row_freq, col_freq, band_rows, total_cols):
    row_sine = jnp.sin(math.pi * row_freq.astype(jnp.float32) / band_rows)
    col_sine = jnp.sin(math.pi * col_freq.astype(jnp.float32) / total_cols)
    inner_term = kappa_sq + 4.0 * row_sine * row_sine + 4.0 * col_sine * col_sine
    symbol = prior_scale * inner_term * inner_term + weight_shift
    quarter = total_cols // 4
    retained = (col_freq < quarter) | (col_freq > total_cols - quarter)
    weight = jnp.where(retained, 1.0 / symbol, 1.0)
    return weight / float(band_rows * total_cols)


def frequency_of(position, outer_len, inner_len):
    return position // inner_len + outer_len * (position % inner_len)


def precondition(grid_field):
    band_rows, block_cols = grid_field.shape
    col_parts = lax.axis_size("cols")
    col_index = lax.axis_index("cols")
    total_cols = block_cols * col_parts
    outer_len, inner_len = split_lengths(total_cols)
    row_cos, row_sin = dft_table(band_rows)
    spectrum = jnp.stack([left_apply(row_cos, grid_field), -left_apply(row_sin, grid_field)])
    whole_lines = lax.all_to_all(spectrum, "cols", split_axis=1, concat_axis=2, tiled=True)
    line_rows = band_rows // col_parts
    spec_real, spec_imag = columns_forward(whole_lines[0], whole_lines[1])
    row_freq = col_index * line_rows + lax.iota(jnp.int32, line_rows)
    col_freq = frequency_of(lax.iota(jnp.int32, total_cols), outer_len, inner_len)
    spectral_scale = inverse_symbol(row_freq[:, None], col_freq[None, :], band_rows, total_cols)
    back_real, back_imag = columns_inverse(spec_real * spectral_scale, spec_imag * spectral_scale)
    blocks = lax.all_to_all(
        jnp.stack([back_real, back_imag]), "cols", split_axis=2, concat_axis=1, tiled=True
    )
    return left_apply(row_cos, blocks[0]) - left_apply(row_sin, blocks[1])


def prior_apply(grid_field):
    padded = extended(grid_field, (("rows", 0), ("cols", 1)), 2)
    row_count, col_count = grid_field.shape

    def offset_view(shift_row, shift_col):
        return padded[
            2 + shift_row : 2 + shift_row + row_count, 2 + shift_col : 2 + shift_col + col_count
        ]

    centre = kappa_sq + 4.0
    nearest = offset_view(1, 0) + offset_view(-1, 0) + offset_view(0, 1) + offset_view(0, -1)
    diagonal = offset_view(1, 1) + offset_view(1, -1) + offset_view(-1, 1) + offset_view(-1, -1)
    distant = offset_view(2, 0) + offset_view(-2, 0) + offset_view(0, 2) + offset_view(0, -2)
    return prior_scale * (
        (centre * centre + 4.0) * grid_field - 2.0 * centre * nearest + 2.0 * diagonal + distant
    )


def on_device(latent, counts, exposure):
    mean_rate = exposure.astype(jnp.float32) * jnp.exp(latent)
    fisher = dispersion * mean_rate / (dispersion + mean_rate)
    score = (counts.astype(jnp.float32) - mean_rate) * dispersion / (dispersion + mean_rate)
    gradient = score - prior_apply(latent)
    first_search = precondition(gradient)
    first_product = lax.psum(jnp.sum(gradient * first_search), ("rows", "cols"))
    image = prior_apply(first_search) + fisher * first_search
    curvature = lax.psum(jnp.sum(first_search * image), ("rows", "cols"))
    step_size = first_product / curvature
    residual = gradient - step_size * image
    next_search = precondition(residual)
    next_product = lax.psum(jnp.sum(residual * next_search), ("rows", "cols"))
    newton_step = step_size * first_search
    direction = next_search + next_product / first_product * first_search
    return (newton_step, residual, direction)


def solution(mesh):
    placed = (P("rows", "cols"), P("rows", "cols"), P("rows", "cols"))
    return jax.shard_map(
        on_device,
        mesh=mesh,
        in_specs=placed,
        out_specs=(P("rows", "cols"), P("rows", "cols"), P("rows", "cols")),
        check_vma=False,
    )
```

profile of v0, /device:TPU:1, one launch (start us, length us, event | category | flops | bytes accessed | tf_op | source)
XLA Modules:
  0.0 564.2 jit_solution(15677637600210697787)
XLA Ops:
  1.5 5.1 collective-permute-start
  11.9 4.0 collective-permute-start.3
  18.4 2.9 fusion.34
  24.6 9.9 %all-to-all-start = ((f32[2,64,2048]{2,0,1:T(2,128)}), f32[2,64,2048]{2,0,1:T(2,128)S(1)}, u32[]{:S(2)}, u32[]{:S(2)}) async-start(f32[2,64,2048]{2,0,1:T(2,128)} %copy.128), calls=%async_computation | async-start | bytes 2097152 | tf_op jit(solution)/shard_map/all_to_all | solution.py:120
  35.6 27.9 %all-to-all-done = f32[2,64,2048]{2,0,1:T(2,128)S(1)} async-done(((f32[2,64,2048]{2,0,1:T(2,128)}), f32[2,64,2048]{2,0,1:T(2,128)S(1)}, u32[]{:S(2)}, u32[]{:S(2)}) %all-to-all-start) | async-done | bytes 1048608 | tf_op jit(solution)/shard_map/all_to_all | solution.py:120
  83.7 14.7 %copy.146 = f32[2,8,16384]{1,0,2:T(2,128)} copy(f32[2,8,16384]{2,1,0:T(8,128)S(1)} %pad_maximum_fusion.1) | data formatting | bytes 2097152 | tf_op jit(solution)/shard_map/stack | solution.py:128
  98.4 28.3 %reshape.237 = f32[8,1,32768]{2,1,0:T(1,128)S(1)} reshape(f32[16384,2,8]{2,1,0:T(2,128)} %bitcast.148) | data formatting | bytes 2097152
  126.7 31.4 %all_to_all.60 = f32[8,1,32768]{2,1,0:T(1,128)S(1)} all-to-all(f32[8,1,32768]{2,1,0:T(1,128)S(1)} %reshape.237), channel_id=1, replica_groups=mesh['rows'=32,'cols'=8] {'cols'}, dimensions={0} | all-to-all | bytes 2097152 | tf_op jit(solution)/shard_map/all_to_all | solution.py:127
  158.7 3.2 reduce
  161.9 32.3 %reshape.238 = f32[16384,2,8]{2,1,0:T(2,128)} reshape(f32[8,32768]{1,0:T(8,128)S(1)} %reduce) | data formatting | bytes 2097152
  194.2 13.2 %copy.194 = f32[2,8,8,2048]{3,2,1,0:T(8,128)S(1)} copy(f32[2,8,8,2048]{1,0,3,2:T(2,128)} %bitcast.149) | data formatting | bytes 2097152 | tf_op jit(solution)/shard_map/all_to_all | solution.py:127
  211.3 2.4 collective-permute-start.4
  213.8 2.6 collective-permute-done.4
  217.8 4.0 collective-permute-start.7
  224.9 79.0 %all-reduce = (f32[]{:T(128)}, f32[]{:T(128)}) all-reduce(f32[]{:T(128)} %get-tuple-element.4, f32[]{:T(128)} %get-tuple-element.3), channel_id=1, replica_groups=mesh['rows'=32,'cols'=8] {'rows','cols'}, use_global_device_ids=true, to_apply=%region_1.2 | all-reduce | flops 2 | bytes 16 | tf_op jit(solution)/shard_map/psum | solution.py:157
  307.6 31.7 %all_to_all.61 = f32[2,64,2048]{2,0,1:T(2,128)S(1)} all-to-all(f32[2,64,2048]{2,0,1:T(2,128)S(1)} %copy.150), channel_id=1, replica_groups=mesh['rows'=32,'cols'=8] {'cols'}, dimensions={1} | all-to-all | bytes 2097152 | tf_op jit(solution)/shard_map/all_to_all | solution.py:120
  356.9 1.9 stack_reshape.15
  361.1 14.7 %copy.166 = f32[2,8,16384]{1,0,2:T(2,128)} copy(f32[2,8,16384]{2,1,0:T(8,128)S(1)} %pad_maximum_fusion.3) | data formatting | bytes 2097152 | tf_op jit(solution)/shard_map/stack | solution.py:128
  375.8 28.3 %reshape.239 = f32[8,1,32768]{2,1,0:T(1,128)S(1)} reshape(f32[16384,2,8]{2,1,0:T(2,128)} %bitcast.150) | data formatting | bytes 2097152
  404.1 28.8 %all_to_all.62 = f32[8,1,32768]{2,1,0:T(1,128)} all-to-all(f32[8,1,32768]{2,1,0:T(1,128)S(1)} %reshape.239), channel_id=1, replica_groups=mesh['rows'=32,'cols'=8] {'cols'}, dimensions={0} | all-to-all | bytes 2097152 | tf_op jit(solution)/shard_map/all_to_all | solution.py:127
  432.9 4.4 reduce.1
  437.3 32.1 %reshape.240 = f32[16384,2,8]{2,1,0:T(2,128)} reshape(f32[8,32768]{1,0:T(8,128)S(1)} %reduce.1) | data formatting | bytes 2097152
  469.4 13.2 %copy.195 = f32[2,8,8,2048]{3,2,1,0:T(8,128)S(1)} copy(f32[2,8,8,2048]{1,0,3,2:T(2,128)} %bitcast.151) | data formatting | bytes 2097152 | tf_op jit(solution)/shard_map/all_to_all | solution.py:127
  485.2 76.5 %psum.23 = f32[]{:T(128)} all-reduce(f32[]{:T(128)} %get-tuple-element.30), channel_id=1, replica_groups=mesh['rows'=32,'cols'=8] {'rows','cols'}, use_global_device_ids=true, to_apply=%region_5.6 | all-reduce | flops 1 | bytes 8 | tf_op jit(solution)/shard_map/psum | solution.py:163
  (99 shorter events, 67.7 us)
Async XLA Ops:
  1.5 8.2 %collective-permute-start = (f32[2,2048]{1,0:T(2,128)S(1)}, f32[2,2048]{1,0:T(2,128)S(1)}, u32[]{:S(2)}, u32[]{:S(2)}) collective-permute-start(f32[2,2048]{1,0:T(2,128)S(1)} %get-tuple-element.28), channel_id=1, source_target_pairs={{8,0},{16,8},{24,16},{32,24},{40,32},{48,40},{56,48},{64,56},{72,6... | collective-permute-start | bytes 49160 | tf_op jit(solution)/shard_map/ppermute | solution.py:24
  6.7 3.1 collective-permute-start.1
  10.6 5.3 collective-permute-start.2
  11.9 5.0 collective-permute-start.3
  24.6 38.8 %all-to-all-start = ((f32[2,64,2048]{2,0,1:T(2,128)}), f32[2,64,2048]{2,0,1:T(2,128)S(1)}, u32[]{:S(2)}, u32[]{:S(2)}) async-start(f32[2,64,2048]{2,0,1:T(2,128)} %copy.128), calls=%async_computation | async-start | bytes 2097152 | tf_op jit(solution)/shard_map/all_to_all | solution.py:120
  194.2 28.9 %copy-start = (f32[64,2048]{1,0:T(8,128)S(1)}, f32[64,2048]{1,0:T(8,128)}, u32[]{:S(2)}) copy-start(f32[64,2048]{1,0:T(8,128)} %param.3) | copy-start | bytes 1572868
  194.2 28.9 %copy-start.2 = (s32[64,2048]{1,0:T(8,128)S(1)}, s32[64,2048]{1,0:T(8,128)}, u32[]{:S(2)}) copy-start(s32[64,2048]{1,0:T(8,128)} %param.5) | copy-start | bytes 1572868
  209.4 4.3 collective-permute-start.5
  211.3 5.1 collective-permute-start.4
  216.5 5.3 collective-permute-start.6
  217.8 5.0 collective-permute-start.7
  305.3 178.3 %copy-start.1 = (f32[64,2048]{1,0:T(8,128)}, f32[64,2048]{1,0:T(8,128)S(1)}, u32[]{:S(2)}) copy-start(f32[64,2048]{1,0:T(8,128)S(1)} %multiply_subtract_fusion.2) | copy-start | bytes 1572868
where the time goes:
time: 569 us; the launch traced here: 564 us
  blocking collectives  247 us (43%)
  local copies, waits for them, and re-layouts  189 us (33%)
  matrix products  40.4 us (7%)
  waiting for transfers between devices  32.6 us (6%)
  starting transfers between devices  31.8 us (6%)
  other arithmetic  19.3 us (3%)
    unnamed x11, local copies, waits for them, and re-layouts  122 us
    psum x1, blocking collectives, on_device(): first_product = lax.psum(jnp.sum(gradient * first_search), ('rows', 'cols'))  79 us
    psum x1, blocking collectives, on_device(): next_product = lax.psum(jnp.sum(residual * next_search), ('rows', 'cols'))  76.5 us
    all_to_all x2, blocking collectives, precondition(): lax.all_to_all(jnp.stack([back_real, back_imag]), 'cols', split_axis=2, c...  60.2 us
    another operation x6, local copies, waits for them, and re-layouts, precondition(): jnp.stack([back_real, back_imag])  32.4 us
    all_to_all x1, blocking collectives, precondition(): lax.all_to_all(spectrum, 'cols', split_axis=1, concat_axis=2, tiled=True)  31.7 us
    all_to_all x1, waiting for transfers between devices, precondition(): lax.all_to_all(spectrum, 'cols', split_axis=1, concat_axis=2, tiled=True)  27.9 us
    all_to_all x3, local copies, waits for them, and re-layouts, precondition(): lax.all_to_all(jnp.stack([back_real, back_imag]), 'cols', split_axis=2, c...  27 us
  transfers between devices with their start and end apart: 9, of which 5 were waited for; matrix products, arithmetic and copies ran while one was open for 0% of the time, Pallas kernels for 0%

commit v1 on v0

--- a/solution.py
+++ b/solution.py
@@ -9,6 +9,30 @@
 kappa_sq = 0.05
 weight_shift = 1.0
 highest = lax.Precision.HIGHEST
+
+
+def split_up(x, dim, size):
+    shape = x.shape
+    pieces = x.reshape(*shape[:dim], size, shape[dim] // size, *shape[dim + 1 :])
+    return jnp.moveaxis(pieces, dim, 0)
+
+
+def laid_out(blocks, dim):
+    shape = list(blocks.shape[1:])
+    shape[dim] *= blocks.shape[0]
+    return jnp.moveaxis(blocks, 0, dim).reshape(shape)
+
+
+def sent_to_each(array, axis, split_dim, concat_dim):
+    length, place = (lax.axis_size(axis), lax.axis_index(axis))
+    blocks = split_up(array, split_dim, length)
+    whole = blocks
+    for step in range(1, length):
+        target, source = ((place + step) % length, (place - step) % length)
+        sent = lax.dynamic_index_in_dim(blocks, target, 0)
+        received = lax.ppermute(sent, axis, [(i, (i + step) % length) for i in range(length)])
+        whole = lax.dynamic_update_slice_in_dim(whole, received, source, axis=0)
+    return laid_out(whole, concat_dim)
 
 
 def extended(cells, sides, width):
@@ -124,9 +148,7 @@
     col_freq = frequency_of(lax.iota(jnp.int32, total_cols), outer_len, inner_len)
     spectral_scale = inverse_symbol(row_freq[:, None], col_freq[None, :], band_rows, total_cols)
     back_real, back_imag = columns_inverse(spec_real * spectral_scale, spec_imag * spectral_scale)
-    blocks = lax.all_to_all(
-        jnp.stack([back_real, back_imag]), "cols", split_axis=2, concat_axis=1, tiled=True
-    )
+    blocks = sent_to_each(jnp.stack([back_real, back_imag]), "cols", 2, 1)
     return left_apply(row_cos, blocks[0]) - left_apply(row_sin, blocks[1])
 
 

time: 569 us -> 390 us (0.69)
  local copies, waits for them, and re-layouts: 189 us -> 40 us
  blocking collectives: 247 us -> 187 us
  starting transfers between devices: 31.8 us -> 52 us
  waiting for transfers between devices: 32.6 us -> 52 us
  other arithmetic: 19.3 us -> 5.89 us
    unnamed x11 -> x29, local copies, waits for them, and re-layouts: 122 us -> 4.49 us
    all_to_all x2 -> x0, blocking collectives: 60.2 us -> none  [precondition(): lax.all_to_all(jnp.stack([back_real, back_imag]), 'cols', split_axis=2, c...]
    another operation x6, local copies, waits for them, and re-layouts: 32.4 us -> 4.07 us  [precondition(): blocks = sent_to_each(jnp.stack([back_real, back_imag]), 'cols', 2, 1)]
    all_to_all x3 -> x0, local copies, waits for them, and re-layouts: 27 us -> none  [precondition(): lax.all_to_all(jnp.stack([back_real, back_imag]), 'cols', split_axis=2, c...]
    ppermute x0 -> x14, starting transfers between devices: none -> 20 us  [sent_to_each(): lax.ppermute(sent, axis, [(i, (i + step) % length) for i in range(length)])]
    ppermute x0 -> x14, waiting for transfers between devices: none -> 19.6 us  [sent_to_each(): lax.ppermute(sent, axis, [(i, (i + step) % length) for i in range(length)])]
    dynamic_update_slice x0 -> x14, local copies, waits for them, and re-layouts: none -> 19.5 us  [sent_to_each(): whole = lax.dynamic_update_slice_in_dim(whole, received, source, axis=0)]
    all_to_all x2 -> x0, other arithmetic: 7.58 us -> none  [precondition(): lax.all_to_all(jnp.stack([back_real, back_imag]), 'cols', split_axis=2, c...]
  transfers between devices with their start and end apart: 9 -> 23, of which waited for: 5 -> 9; matrix products, arithmetic and copies ran while one was open for 0% -> 5% of each run, Pallas kernels for 0% -> 0%
where the time goes in v1:
time: 390 us; the launch traced here: 384 us
  blocking collectives  187 us (48%)
  starting transfers between devices  52 us (13%)
  waiting for transfers between devices  52 us (13%)
  matrix products  42.2 us (11%)
  local copies, waits for them, and re-layouts  40 us (10%)
  other arithmetic  5.89 us (2%)
  between operations  4.44 us (1%)
    psum x1, blocking collectives, on_device(): first_product = lax.psum(jnp.sum(gradient * first_search), ('rows', 'cols'))  79.6 us
    psum x1, blocking collectives, on_device(): next_product = lax.psum(jnp.sum(residual * next_search), ('rows', 'cols'))  75.8 us
    all_to_all x1, blocking collectives, precondition(): lax.all_to_all(spectrum, 'cols', split_axis=1, concat_axis=2, tiled=True)  32 us
    all_to_all x1, waiting for transfers between devices, precondition(): lax.all_to_all(spectrum, 'cols', split_axis=1, concat_axis=2, tiled=True)  27.7 us
    ppermute x14, starting transfers between devices, sent_to_each(): lax.ppermute(sent, axis, [(i, (i + step) % length) for i in range(length)])  20 us
    ppermute x14, waiting for transfers between devices, sent_to_each(): lax.ppermute(sent, axis, [(i, (i + step) % length) for i in range(length)])  19.6 us
    dynamic_update_slice x14, local copies, waits for them, and re-layouts, sent_to_each(): whole = lax.dynamic_update_slice_in_dim(whole, received, source, axis=0)  19.5 us
    dot_general x16, matrix products, last_apply(): jnp.dot(data.reshape(line_rows * outer_len, inner_len), table, precision=...  17.8 us
  transfers between devices with their start and end apart: 23, of which 9 were waited for; matrix products, arithmetic and copies ran while one was open for 5% of the time, Pallas kernels for 0%

profile of v1, /device:TPU:1, one launch (start us, length us, event | category | flops | bytes accessed | tf_op | source)
XLA Modules:
  0.0 384.1 jit_solution(5879156798381828356)
XLA Ops:
  1.5 5.1 %collective-permute-start = (f32[2,2048]{1,0:T(2,128)S(1)}, f32[2,2048]{1,0:T(2,128)S(1)}, u32[]{:S(2)}, u32[]{:S(2)}) collective-permute-start(f32[2,2048]{1,0:T(2,128)S(1)} %get-tuple-element.42), channel_id=1, source_target_pairs={{8,0},{16,8},{24,16},{32,24},{40,32},{48,40},{56,48},{64,56},{72,6... | collective-permute-start | bytes 49160 | tf_op jit(solution)/shard_map/ppermute | solution.py:48
  6.7 2.1 collective-permute-start.1
  11.3 4.0 %collective-permute-start.3 = (f32[68,2]{1,0:T(8,128)S(1)}, f32[68,2]{1,0:T(8,128)S(1)}, u32[]{:S(2)}, u32[]{:S(2)}) collective-permute-start(f32[68,2]{1,0:T(8,128)S(1)} %get-tuple-element.37), channel_id=1, source_target_pairs={{0,1},{1,2},{2,3},{3,4},{4,5},{5,6},{6,7},{8,9},{9,10},{10,11},{11... | collective-permute-start | bytes 1640 | tf_op jit(solution)/shard_map/ppermute | solution.py:46
  21.1 9.9 %all-to-all-start = ((f32[2,64,2048]{2,0,1:T(2,128)}), f32[2,64,2048]{2,0,1:T(2,128)S(1)}, u32[]{:S(2)}, u32[]{:S(2)}) async-start(f32[2,64,2048]{2,0,1:T(2,128)} %copy.60), calls=%async_computation | async-start | bytes 2097152 | tf_op jit(solution)/shard_map/all_to_all | solution.py:144
  32.3 27.7 %all-to-all-done = f32[2,64,2048]{2,0,1:T(2,128)S(1)} async-done(((f32[2,64,2048]{2,0,1:T(2,128)}), f32[2,64,2048]{2,0,1:T(2,128)S(1)}, u32[]{:S(2)}, u32[]{:S(2)}) %all-to-all-start) | async-done | bytes 1048608 | tf_op jit(solution)/shard_map/all_to_all | solution.py:144
  77.7 2.0 copy.77
  86.8 4.7 %collective-permute-start.8 = (f32[1,2,8,2048]{3,0,2,1:T(1,128)S(1)}, f32[1,2,8,2048]{3,0,2,1:T(1,128)S(1)}, u32[]{:S(2)}, u32[]{:S(2)}) collective-permute-start(f32[1,2,8,2048]{3,0,2,1:T(1,128)S(1)} %get-tuple-element.23), channel_id=1, source_target_pairs={{0,5},{1,6},{2,7},{3,0},{4,1},{5,2},{6,3},{7,4},{8,13},{9,14},{10,... | collective-permute-start | bytes 393224 | tf_op jit(solution)/shard_map/ppermute | solution.py:33
  93.5 2.7 collective-permute-start.9
  97.2 2.0 dynamic_update_slice.42
  99.2 2.1 dynamic_update_slice.43
  101.3 2.1 dynamic_update_slice.44
  103.4 8.7 %collective-permute-done.7 = f32[1,2,8,2048]{3,0,2,1:T(1,128)} collective-permute-done((f32[1,2,8,2048]{3,0,2,1:T(1,128)S(1)}, f32[1,2,8,2048]{3,0,2,1:T(1,128)}, u32[]{:S(2)}, u32[]{:S(2)}) %collective-permute-start.7) | collective-permute-done | bytes 131104 | tf_op jit(solution)/shard_map/ppermute | solution.py:33
  112.1 2.0 dynamic_update_slice.45
  114.9 2.1 dynamic_update_slice.47
  117.0 2.1 dynamic_update_slice.48
  122.9 2.4 collective-permute-start.11
  125.4 2.6 collective-permute-done.11
  129.4 4.1 %collective-permute-start.14 = (f32[68,2]{1,0:T(8,128)S(1)}, f32[68,2]{1,0:T(8,128)S(1)}, u32[]{:S(2)}, u32[]{:S(2)}) collective-permute-start(f32[68,2]{1,0:T(8,128)S(1)} %get-tuple-element.33), channel_id=1, source_target_pairs={{0,1},{1,2},{2,3},{3,4},{4,5},{5,6},{6,7},{8,9},{9,10},{10,11},{11... | collective-permute-start | bytes 1640 | tf_op jit(solution)/shard_map/ppermute | solution.py:46
  136.6 79.6 %all-reduce = (f32[]{:T(128)}, f32[]{:T(128)}) all-reduce(f32[]{:T(128)} %get-tuple-element.4, f32[]{:T(128)} %get-tuple-element.3), channel_id=1, replica_groups=mesh['rows'=32,'cols'=8] {'rows','cols'}, use_global_device_ids=true, to_apply=%region_1.2 | all-reduce | flops 2 | bytes 16 | tf_op jit(solution)/shard_map/psum | solution.py:179
  220.0 32.0 %all_to_all.30 = f32[2,64,2048]{2,0,1:T(2,128)S(1)} all-to-all(f32[2,64,2048]{2,0,1:T(2,128)S(1)} %copy.80), channel_id=1, replica_groups=mesh['rows'=32,'cols'=8] {'cols'}, dimensions={1} | all-to-all | bytes 2097152 | tf_op jit(solution)/shard_map/all_to_all | solution.py:144
  275.9 3.8 collective-permute-start.19
  281.8 2.8 collective-permute-start.20
  290.2 9.3 %collective-permute-done.18 = f32[1,2,8,2048]{3,0,2,1:T(1,128)S(1)} collective-permute-done((f32[1,2,8,2048]{3,0,2,1:T(1,128)S(1)}, f32[1,2,8,2048]{3,0,2,1:T(1,128)S(1)}, u32[]{:S(2)}, u32[]{:S(2)}) %collective-permute-start.18) | collective-permute-done | bytes 131104 | tf_op jit(solution)/shard_map/ppermute | solution.py:33
  305.7 75.8 %psum.23 = f32[]{:T(128)} all-reduce(f32[]{:T(128)} %get-tuple-element.44), channel_id=1, replica_groups=mesh['rows'=32,'cols'=8] {'rows','cols'}, use_global_device_ids=true, to_apply=%region_5.6 | all-reduce | flops 1 | bytes 8 | tf_op jit(solution)/shard_map/psum | solution.py:185
  (152 shorter events, 88.0 us)
Async XLA Ops:
  1.5 8.3 %collective-permute-start = (f32[2,2048]{1,0:T(2,128)S(1)}, f32[2,2048]{1,0:T(2,128)S(1)}, u32[]{:S(2)}, u32[]{:S(2)}) collective-permute-start(f32[2,2048]{1,0:T(2,128)S(1)} %get-tuple-element.42), channel_id=1, source_target_pairs={{8,0},{16,8},{24,16},{32,24},{40,32},{48,40},{56,48},{64,56},{72,6... | collective-permute-start | bytes 49160 | tf_op jit(solution)/shard_map/ppermute | solution.py:48
  6.7 3.2 collective-permute-start.1
  10.0 5.3 %collective-permute-start.2 = (f32[68,2]{1,0:T(8,128)S(1)}, f32[68,2]{1,0:T(8,128)S(1)}, u32[]{:S(2)}, u32[]{:S(2)}) collective-permute-start(f32[68,2]{1,0:T(8,128)S(1)} %get-tuple-element.36), channel_id=1, source_target_pairs={{1,0},{2,1},{3,2},{4,3},{5,4},{6,5},{7,6},{9,8},{10,9},{11,10},{12... | collective-permute-start | bytes 1640 | tf_op jit(solution)/shard_map/ppermute | solution.py:48
  11.3 5.0 %collective-permute-start.3 = (f32[68,2]{1,0:T(8,128)S(1)}, f32[68,2]{1,0:T(8,128)S(1)}, u32[]{:S(2)}, u32[]{:S(2)}) collective-permute-start(f32[68,2]{1,0:T(8,128)S(1)} %get-tuple-element.37), channel_id=1, source_target_pairs={{0,1},{1,2},{2,3},{3,4},{4,5},{5,6},{6,7},{8,9},{9,10},{10,11},{11... | collective-permute-start | bytes 1640 | tf_op jit(solution)/shard_map/ppermute | solution.py:46
  21.1 38.9 %all-to-all-start = ((f32[2,64,2048]{2,0,1:T(2,128)}), f32[2,64,2048]{2,0,1:T(2,128)S(1)}, u32[]{:S(2)}, u32[]{:S(2)}) async-start(f32[2,64,2048]{2,0,1:T(2,128)} %copy.60), calls=%async_computation | async-start | bytes 2097152 | tf_op jit(solution)/shard_map/all_to_all | solution.py:144
  86.6 6.8 %collective-permute-start.5 = (f32[1,2,8,2048]{3,0,2,1:T(1,128)S(1)}, f32[1,2,8,2048]{3,0,2,1:T(1,128)S(1)}, u32[]{:S(2)}, u32[]{:S(2)}) collective-permute-start(f32[1,2,8,2048]{3,0,2,1:T(1,128)S(1)} %get-tuple-element.26), channel_id=1, source_target_pairs={{0,2},{1,3},{2,4},{3,5},{4,6},{5,7},{6,0},{7,1},{8,10},{9,11},{10,... | collective-permute-start | bytes 393224 | tf_op jit(solution)/shard_map/ppermute | solution.py:33
  86.7 9.4 %collective-permute-start.4 = (f32[1,2,8,2048]{3,0,2,1:T(1,128)S(1)}, f32[1,2,8,2048]{3,0,2,1:T(1,128)S(1)}, u32[]{:S(2)}, u32[]{:S(2)}) collective-permute-start(f32[1,2,8,2048]{3,0,2,1:T(1,128)S(1)} %get-tuple-element.27), channel_id=1, source_target_pairs={{0,1},{1,2},{2,3},{3,4},{4,5},{5,6},{6,7},{7,0},{8,9},{9,10},{10,1... | collective-permute-start | bytes 393224 | tf_op jit(solution)/shard_map/ppermute | solution.py:33
  86.8 27.3 %collective-permute-start.8 = (f32[1,2,8,2048]{3,0,2,1:T(1,128)S(1)}, f32[1,2,8,2048]{3,0,2,1:T(1,128)S(1)}, u32[]{:S(2)}, u32[]{:S(2)}) collective-permute-start(f32[1,2,8,2048]{3,0,2,1:T(1,128)S(1)} %get-tuple-element.23), channel_id=1, source_target_pairs={{0,5},{1,6},{2,7},{3,0},{4,1},{5,2},{6,3},{7,4},{8,13},{9,14},{10,... | collective-permute-start | bytes 393224 | tf_op jit(solution)/shard_map/ppermute | solution.py:33
  91.5 9.8 %collective-permute-start.6 = (f32[1,2,8,2048]{3,0,2,1:T(1,128)S(1)}, f32[1,2,8,2048]{3,0,2,1:T(1,128)}, u32[]{:S(2)}, u32[]{:S(2)}) collective-permute-start(f32[1,2,8,2048]{3,0,2,1:T(1,128)S(1)} %get-tuple-element.25), channel_id=1, source_target_pairs={{0,3},{1,4},{2,5},{3,6},{4,7},{5,0},{6,1},{7,2},{8,11},{9,12},{10,... | collective-permute-start | bytes 393224 | tf_op jit(solution)/shard_map/ppermute | solution.py:33
  91.5 20.6 %collective-permute-start.7 = (f32[1,2,8,2048]{3,0,2,1:T(1,128)S(1)}, f32[1,2,8,2048]{3,0,2,1:T(1,128)}, u32[]{:S(2)}, u32[]{:S(2)}) collective-permute-start(f32[1,2,8,2048]{3,0,2,1:T(1,128)S(1)} %get-tuple-element.24), channel_id=1, source_target_pairs={{0,4},{1,5},{2,6},{3,7},{4,0},{5,1},{6,2},{7,3},{8,12},{9,13},{10,... | collective-permute-start | bytes 393224 | tf_op jit(solution)/shard_map/ppermute | solution.py:33
  93.5 21.4 %collective-permute-start.9 = (f32[1,2,8,2048]{3,0,2,1:T(1,128)S(1)}, f32[1,2,8,2048]{3,0,2,1:T(1,128)}, u32[]{:S(2)}, u32[]{:S(2)}) collective-permute-start(f32[1,2,8,2048]{3,0,2,1:T(1,128)S(1)} %get-tuple-element.22), channel_id=1, source_target_pairs={{0,6},{1,7},{2,0},{3,1},{4,2},{5,3},{6,4},{7,5},{8,14},{9,15},{10,... | collective-permute-start | bytes 393224 | tf_op jit(solution)/shard_map/ppermute | solution.py:33
  96.8 20.2 %collective-permute-start.10 = (f32[1,2,8,2048]{3,0,2,1:T(1,128)S(1)}, f32[1,2,8,2048]{3,0,2,1:T(1,128)}, u32[]{:S(2)}, u32[]{:S(2)}) collective-permute-start(f32[1,2,8,2048]{3,0,2,1:T(1,128)S(1)} %get-tuple-element.21), channel_id=1, source_target_pairs={{0,7},{1,0},{2,1},{3,2},{4,3},{5,4},{6,5},{7,6},{8,15},{9,8},{10,9... | collective-permute-start | bytes 393224 | tf_op jit(solution)/shard_map/ppermute | solution.py:33
  121.0 4.3 %collective-permute-start.12 = (f32[2,2048]{1,0:T(2,128)S(1)}, f32[2,2048]{1,0:T(2,128)S(1)}, u32[]{:S(2)}, u32[]{:S(2)}) collective-permute-start(f32[2,2048]{1,0:T(2,128)S(1)} %get-tuple-element.40), channel_id=1, source_target_pairs={{0,8},{8,16},{16,24},{24,32},{32,40},{40,48},{48,56},{56,64},{64,7... | collective-permute-start | bytes 49160 | tf_op jit(solution)/shard_map/ppermute | solution.py:46
  122.9 5.1 %collective-permute-start.11 = (f32[2,2048]{1,0:T(2,128)S(1)}, f32[2,2048]{1,0:T(2,128)S(1)}, u32[]{:S(2)}, u32[]{:S(2)}) collective-permute-start(f32[2,2048]{1,0:T(2,128)S(1)} %get-tuple-element.41), channel_id=1, source_target_pairs={{8,0},{16,8},{24,16},{32,24},{40,32},{48,40},{56,48},{64,56},{72,6... | collective-permute-start | bytes 49160 | tf_op jit(solution)/shard_map/ppermute | solution.py:48
  128.1 5.4 %collective-permute-start.13 = (f32[68,2]{1,0:T(8,128)S(1)}, f32[68,2]{1,0:T(8,128)S(1)}, u32[]{:S(2)}, u32[]{:S(2)}) collective-permute-start(f32[68,2]{1,0:T(8,128)S(1)} %get-tuple-element.32), channel_id=1, source_target_pairs={{1,0},{2,1},{3,2},{4,3},{5,4},{6,5},{7,6},{9,8},{10,9},{11,10},{12... | collective-permute-start | bytes 1640 | tf_op jit(solution)/shard_map/ppermute | solution.py:48
  129.4 5.1 %collective-permute-start.14 = (f32[68,2]{1,0:T(8,128)S(1)}, f32[68,2]{1,0:T(8,128)S(1)}, u32[]{:S(2)}, u32[]{:S(2)}) collective-permute-start(f32[68,2]{1,0:T(8,128)S(1)} %get-tuple-element.33), channel_id=1, source_target_pairs={{0,1},{1,2},{2,3},{3,4},{4,5},{5,6},{6,7},{8,9},{9,10},{10,11},{11... | collective-permute-start | bytes 1640 | tf_op jit(solution)/shard_map/ppermute | solution.py:46
  217.6 86.6 %copy-start.1 = (f32[64,2048]{1,0:T(8,128)}, f32[64,2048]{1,0:T(8,128)S(1)}, u32[]{:S(2)}) copy-start(f32[64,2048]{1,0:T(8,128)S(1)} %multiply_subtract_fusion.2) | copy-start | bytes 1572868
  274.9 6.8 %collective-permute-start.16 = (f32[1,2,8,2048]{3,0,2,1:T(1,128)S(1)}, f32[1,2,8,2048]{3,0,2,1:T(1,128)S(1)}, u32[]{:S(2)}, u32[]{:S(2)}) collective-permute-start(f32[1,2,8,2048]{3,0,2,1:T(1,128)S(1)} %get-tuple-element.15), channel_id=1, source_target_pairs={{0,2},{1,3},{2,4},{3,5},{4,6},{5,7},{6,0},{7,1},{8,10},{9,11},{10,... | collective-permute-start | bytes 393224 | tf_op jit(solution)/shard_map/ppermute | solution.py:33
  275.0 9.5 %collective-permute-start.15 = (f32[1,2,8,2048]{3,0,2,1:T(1,128)S(1)}, f32[1,2,8,2048]{3,0,2,1:T(1,128)S(1)}, u32[]{:S(2)}, u32[]{:S(2)}) collective-permute-start(f32[1,2,8,2048]{3,0,2,1:T(1,128)S(1)} %get-tuple-element.16), channel_id=1, source_target_pairs={{0,1},{1,2},{2,3},{3,4},{4,5},{5,6},{6,7},{7,0},{8,9},{9,10},{10,1... | collective-permute-start | bytes 393224 | tf_op jit(solution)/shard_map/ppermute | solution.py:33
  275.9 24.3 %collective-permute-start.19 = (f32[1,2,8,2048]{3,0,2,1:T(1,128)S(1)}, f32[1,2,8,2048]{3,0,2,1:T(1,128)S(1)}, u32[]{:S(2)}, u32[]{:S(2)}) collective-permute-start(f32[1,2,8,2048]{3,0,2,1:T(1,128)S(1)} %get-tuple-element.12), channel_id=1, source_target_pairs={{0,5},{1,6},{2,7},{3,0},{4,1},{5,2},{6,3},{7,4},{8,13},{9,14},{10,... | collective-permute-start | bytes 393224 | tf_op jit(solution)/shard_map/ppermute | solution.py:33
  279.8 9.7 %collective-permute-start.17 = (f32[1,2,8,2048]{3,0,2,1:T(1,128)S(1)}, f32[1,2,8,2048]{3,0,2,1:T(1,128)S(1)}, u32[]{:S(2)}, u32[]{:S(2)}) collective-permute-start(f32[1,2,8,2048]{3,0,2,1:T(1,128)S(1)} %get-tuple-element.14), channel_id=1, source_target_pairs={{0,3},{1,4},{2,5},{3,6},{4,7},{5,0},{6,1},{7,2},{8,11},{9,12},{10,... | collective-permute-start | bytes 393224 | tf_op jit(solution)/shard_map/ppermute | solution.py:33
  279.8 19.8 %collective-permute-start.18 = (f32[1,2,8,2048]{3,0,2,1:T(1,128)S(1)}, f32[1,2,8,2048]{3,0,2,1:T(1,128)S(1)}, u32[]{:S(2)}, u32[]{:S(2)}) collective-permute-start(f32[1,2,8,2048]{3,0,2,1:T(1,128)S(1)} %get-tuple-element.13), channel_id=1, source_target_pairs={{0,4},{1,5},{2,6},{3,7},{4,0},{5,1},{6,2},{7,3},{8,12},{9,13},{10,... | collective-permute-start | bytes 393224 | tf_op jit(solution)/shard_map/ppermute | solution.py:33
  281.8 19.3 %collective-permute-start.20 = (f32[1,2,8,2048]{3,0,2,1:T(1,128)S(1)}, f32[1,2,8,2048]{3,0,2,1:T(1,128)S(1)}, u32[]{:S(2)}, u32[]{:S(2)}) collective-permute-start(f32[1,2,8,2048]{3,0,2,1:T(1,128)S(1)} %get-tuple-element.11), channel_id=1, source_target_pairs={{0,6},{1,7},{2,0},{3,1},{4,2},{5,3},{6,4},{7,5},{8,14},{9,15},{10,... | collective-permute-start | bytes 393224 | tf_op jit(solution)/shard_map/ppermute | solution.py:33
  285.2 17.2 %collective-permute-start.21 = (f32[1,2,8,2048]{3,0,2,1:T(1,128)S(1)}, f32[1,2,8,2048]{3,0,2,1:T(1,128)S(1)}, u32[]{:S(2)}, u32[]{:S(2)}) collective-permute-start(f32[1,2,8,2048]{3,0,2,1:T(1,128)S(1)} %get-tuple-element.10), channel_id=1, source_target_pairs={{0,7},{1,0},{2,1},{3,2},{4,3},{5,4},{6,5},{7,6},{8,15},{9,8},{10,9... | collective-permute-start | bytes 393224 | tf_op jit(solution)/shard_map/ppermute | solution.py:33
  (12 other events, 90.0 us)
